TPU v7x, 768 devices: a whole 4x8x12 slice. The times are simulated.
768 devices in a mesh: shot: 24 (over x_lo, z), gx: 4 (over x_hi, core), gy: 8 (over y).
Axes of the slice: x: 4 (x_hi: 2, x_lo: 2; x = x_hi * 2 + x_lo), y: 8, z: 12, core: 2. Of those that a mesh axis runs over, the one named last changes fastest.
Arguments:
- partials: float32 [24, 9, 24, 32, 1024], P('shot', None, None, 'gx', 'gy'), may hold values from -16 to 16, as said below
- hist_s: float32 [5, 3, 24, 32, 1024], P(None, None, 'shot', 'gx', 'gy'), may hold values from -30 to 30
- hist_y: float32 [5, 3, 24, 32, 1024], P(None, None, 'shot', 'gx', 'gy'), may hold values from -70 to 70, as said below
Outputs:
- direction: float32 [3, 24, 32, 1024], P(None, 'shot', 'gx', 'gy')
Inputs may be any that keep to these rules, and one draw needn't show every extreme that they name: `partials`: for every shot group and cell, entries 3, 4, 5 are positive and each exceeds the sum of the magnitudes of the two off-diagonal entries of its row of the 3x3 matrix [[e3, e6, e7], [e6, e4, e8], [e7, e8, e5]]. Each entry of hist_y times the matching entry of hist_s is at least 0.2 times the square of that hist_s entry.
All inputs are finite; a program needn't handle non-finite values.
Results may differ from a plain program's by a relative error of at most 0.00013.
Values sent between devices are 32-bit elements; how exact they have to be, the bound alone decides.
A program may use at most 32 MiB of HBM per device.

v0:
```python
import jax
import jax.numpy as jnp
from jax import lax
from jax.sharding import PartitionSpec as P

PAIRS = 5


def extended_2(cells, sides, width):
    for axis, dim in sides:
        count = lax.axis_size(axis)
        ends = count - 1
        head = lax.slice_in_dim(cells, 0, width, axis=dim)
        tail = lax.slice_in_dim(cells, cells.shape[dim] - width, cells.shape[dim], axis=dim)
        cells = jnp.concatenate(
            [
                lax.ppermute(tail, axis, [(i, (i + 1) % count) for i in range(ends)]),
                cells,
                lax.ppermute(head, axis, [((i + 1) % count, i) for i in range(ends)]),
            ],
            axis=dim,
        )
    return cells


def smooth_block(padded):
    along_x = 0.25 * (padded[:, :, :-2] + 2.0 * padded[:, :, 1:-1] + padded[:, :, 2:])
    return 0.25 * (along_x[..., :-2] + 2.0 * along_x[..., 1:-1] + along_x[..., 2:])


def apply_inverse(hessian, vectors):
    diag_p = hessian[0]
    diag_s = hessian[1]
    diag_r = hessian[2]
    cross_ps = hessian[3]
    cross_pr = hessian[4]
    cross_sr = hessian[5]
    cof_pp = diag_s * diag_r - cross_sr * cross_sr
    cof_ps = cross_pr * cross_sr - cross_ps * diag_r
    cof_pr = cross_ps * cross_sr - diag_s * cross_pr
    cof_ss = diag_p * diag_r - cross_pr * cross_pr
    cof_sr = cross_ps * cross_pr - diag_p * cross_sr
    cof_rr = diag_p * diag_s - cross_ps * cross_ps
    determinant = diag_p * cof_pp + cross_ps * cof_ps + cross_pr * cof_pr
    inverse_det = 1.0 / determinant
    comp_one = vectors[:, 0]
    comp_two = vectors[:, 1]
    comp_three = vectors[:, 2]
    return jnp.stack(
        [
            (cof_pp * comp_one + cof_ps * comp_two + cof_pr * comp_three) * inverse_det,
            (cof_ps * comp_one + cof_ss * comp_two + cof_sr * comp_three) * inverse_det,
            (cof_pr * comp_one + cof_sr * comp_two + cof_rr * comp_three) * inverse_det,
        ],
        axis=1,
    )


def pair_dots(left_flat, right_flat):
    return lax.dot_general(
        left_flat,
        right_flat,
        (((1,), (1,)), ((), ())),
        precision=lax.Precision.HIGHEST,
        preferred_element_type=jnp.float32,
    )


def upper_solve(matrix, values):
    count = matrix.shape[0]
    found = [None] * count
    for row in range(count - 1, -1, -1):
        total = values[row]
        for col in range(row + 1, count):
            total = total - matrix[row, col] * found[col]
        found[row] = total / matrix[row, row]
    return jnp.stack(found)


def upper_transpose_solve(matrix, values):
    count = matrix.shape[0]
    found = [None] * count
    for row in range(count):
        total = values[row]
        for col in range(row):
            total = total - matrix[col, row] * found[col]
        found[row] = total / matrix[row, row]
    return jnp.stack(found)


def combine_terms(cross_gram, curv_gram, hist_dot, pre_dot, solved, hist_s):
    middle_part = jnp.diag(jnp.diag(cross_gram)) + curv_gram
    coef_p = upper_solve(cross_gram, hist_dot)
    right_hand = jnp.dot(middle_part, coef_p, precision=lax.Precision.HIGHEST) - pre_dot
    coef_q = upper_transpose_solve(cross_gram, right_hand)
    update_s = jnp.tensordot(coef_q, hist_s, axes=1, precision=lax.Precision.HIGHEST)
    update_z = jnp.tensordot(coef_p, solved[1:], axes=1, precision=lax.Precision.HIGHEST)
    return -(solved[0] + update_s - update_z)


def per_device(partials, hist_s, hist_y):
    levels = hist_s.shape[2]
    s_flat = hist_s.reshape(PAIRS, -1)
    y_flat = hist_y.reshape(PAIRS, -1)
    inverse_count = 1.0 / lax.axis_size("shot")
    totals = lax.psum(partials[0], "shot")
    level_sums = lax.dynamic_slice_in_dim(totals, lax.axis_index("shot") * levels, levels, 1)
    fields = level_sums * inverse_count
    extended = extended_2(fields, (("gx", 2), ("gy", 3)), 1)
    smoothed = smooth_block(extended)
    gradient = smoothed[0:3]
    solved = apply_inverse(smoothed[3:9], jnp.concatenate([gradient[None], hist_y], axis=0))
    z_flat = solved[1:].reshape(PAIRS, -1)
    curv_part = pair_dots(y_flat, z_flat)
    hist_part = pair_dots(s_flat, gradient.reshape(1, -1))[:, 0]
    pre_part = pair_dots(y_flat, solved[0].reshape(1, -1))[:, 0]
    cross_gram, curv_gram, hist_dot, pre_dot = lax.psum(
        (pair_dots(s_flat, y_flat), curv_part, hist_part, pre_part), ("shot", "gx", "gy")
    )
    return combine_terms(cross_gram, curv_gram, hist_dot, pre_dot, solved, hist_s)


def solution(mesh):
    return jax.shard_map(
        per_device,
        mesh=mesh,
        in_specs=(
            P("shot", None, None, "gx", "gy"),
            P(None, None, "shot", "gx", "gy"),
            P(None, None, "shot", "gx", "gy"),
        ),
        out_specs=P(None, "shot", "gx", "gy"),
        check_vma=False,
    )
```

profile of v0, /device:TPU:1, one launch (start us, length us, event | category | flops | bytes accessed | tf_op | source)
XLA Modules:
  0.0 383.8 jit_solution(14942212764841610441)
XLA Ops:
  6.5 0.0 all-reduce.3.cloned.1.call-start
  6.5 2.2 copy.41
  8.7 0.0 all-reduce.3.cloned.1.call-update
  8.8 198.3 %all-reduce.3.cloned.1.call-done = f32[9,24,8,128]{3,2,0,1:T(8,128)} async-done(((f32[9,24,8,128]{3,2,0,1:T(8,128)}), f32[9,24,8,128]{3,2,0,1:T(8,128)}) %all-reduce.3.cloned.1.call-update) | async-done | bytes 884752 | tf_op jit(solution)/shard_map/psum | solution.py:106
  207.1 0.8 dynamic-slice_multiply_fusion
  207.9 18.7 %collective-permute-start.1 = (f32[9,1,1,128]{3,2,0,1:T(1,128)S(1)}, f32[9,1,1,128]{3,2,0,1:T(1,128)S(1)}, u32[]{:S(2)}, u32[]{:S(2)}) collective-permute-start(f32[9,1,1,128]{3,2,0,1:T(1,128)S(1)} %get-tuple-element.25), channel_id=1, source_target_pairs={{8,0},{16,8},{24,16},{9,1},{17,9},{25,17},{10,2},{18,10},{26,18},{... | collective-permute-start | bytes 13832 | tf_op jit(solution)/shard_map/ppermute | solution.py:19
  226.6 4.2 %collective-permute-start = (f32[9,1,1,128]{3,2,0,1:T(1,128)S(1)}, f32[9,1,1,128]{3,2,0,1:T(1,128)S(1)}, u32[]{:S(2)}, u32[]{:S(2)}) collective-permute-start(f32[9,1,1,128]{3,2,0,1:T(1,128)S(1)} %get-tuple-element.24), channel_id=1, source_target_pairs={{0,8},{8,16},{16,24},{1,9},{9,17},{17,25},{2,10},{10,18},{18,26},{... | collective-permute-start | bytes 13832 | tf_op jit(solution)/shard_map/ppermute | solution.py:17
  230.8 0.0 collective-permute-done.1
  230.8 0.7 collective-permute-done
  231.5 0.0 copy-start
  231.5 0.0 copy-start.1
  231.6 0.1 fusion.31
  231.6 1.3 collective-permute-start.3
  232.9 4.0 %collective-permute-start.2 = (f32[9,1,10,1]{3,2,0,1:T(8,128)S(1)}, f32[9,1,10,1]{3,2,0,1:T(8,128)S(1)}, u32[]{:S(2)}, u32[]{:S(2)}) collective-permute-start(f32[9,1,10,1]{3,2,0,1:T(8,128)S(1)} %get-tuple-element.16), channel_id=1, source_target_pairs={{0,1},{1,2},{2,3},{3,4},{4,5},{5,6},{6,7},{8,9},{9,10},{10,11},{11... | collective-permute-start | bytes 1088 | tf_op jit(solution)/shard_map/ppermute | solution.py:17
  236.9 0.0 copy-done
  236.9 0.0 copy-done.1
  237.0 0.3 convolution_bitcast_fusion.1
  237.2 0.0 collective-permute-done.3
  237.2 1.1 collective-permute-done.2
  238.3 0.2 pad_maximum_fusion
  238.5 0.1 fusion.15
  238.7 0.3 convolution_bitcast_fusion.4
  239.0 0.3 convolution_bitcast_fusion
  239.3 0.3 convolution_bitcast_fusion.3
  239.7 0.1 or_bitcast_fusion
  239.7 107.5 %all-reduce = (f32[5]{0:T(128)S(1)}, f32[5,5]{1,0:T(8,128)S(1)}, f32[5]{0:T(128)S(1)}, f32[5,5]{1,0:T(8,128)S(1)}) all-reduce(f32[5]{0:T(128)S(1)} %convolution_bitcast_fusion.4, f32[5,5]{1,0:T(8,128)S(1)} %convolution_bitcast_fusion.1, ...), channel_id=1, replica_groups=mesh['shot'=24,'gx'=4,'gy'=8] {'shot','gx','gy'}, use_global_device_ids=true, to_apply=%region_3.0 | all-reduce | flops 60 | bytes 480 | tf_op jit(solution)/shard_map/psum | solution.py:117
  347.2 0.7 fusion.36
  347.9 0.7 fusion.34
  361.4 0.1 stack.48
  361.5 0.2 fusion.5
  361.7 0.6 gather_fusion
  362.4 0.2 fusion
  362.6 0.7 fusion.35
  376.0 0.1 stack.54
  376.1 0.2 fusion.1
  376.3 0.6 fusion.21
  (9 shorter events, 0.1 us)
Async XLA Ops:
  6.5 200.6 %all-reduce.3.cloned.1.call-start = ((), (), s32[]{:S(2)}) async-start(), calls=%async_computation | async-start | bytes 1769472 | tf_op jit(solution)/shard_map/psum | solution.py:106
  207.9 22.9 %collective-permute-start.1 = (f32[9,1,1,128]{3,2,0,1:T(1,128)S(1)}, f32[9,1,1,128]{3,2,0,1:T(1,128)S(1)}, u32[]{:S(2)}, u32[]{:S(2)}) collective-permute-start(f32[9,1,1,128]{3,2,0,1:T(1,128)S(1)} %get-tuple-element.25), channel_id=1, source_target_pairs={{8,0},{16,8},{24,16},{9,1},{17,9},{25,17},{10,2},{18,10},{26,18},{... | collective-permute-start | bytes 13832 | tf_op jit(solution)/shard_map/ppermute | solution.py:19
  226.6 5.0 %collective-permute-start = (f32[9,1,1,128]{3,2,0,1:T(1,128)S(1)}, f32[9,1,1,128]{3,2,0,1:T(1,128)S(1)}, u32[]{:S(2)}, u32[]{:S(2)}) collective-permute-start(f32[9,1,1,128]{3,2,0,1:T(1,128)S(1)} %get-tuple-element.24), channel_id=1, source_target_pairs={{0,8},{8,16},{16,24},{1,9},{9,17},{17,25},{2,10},{10,18},{18,26},{... | collective-permute-start | bytes 13832 | tf_op jit(solution)/shard_map/ppermute | solution.py:17
  231.5 5.4 %copy-start = (f32[5,3,1,8,128]{4,3,2,1,0:T(8,128)S(1)}, f32[5,3,1,8,128]{4,3,2,1,0:T(8,128)}, u32[]{:S(2)}) copy-start(f32[5,3,1,8,128]{4,3,2,1,0:T(8,128)} %param.5) | copy-start | bytes 184324
  231.5 5.4 %copy-start.1 = (f32[5,3,1,8,128]{4,3,2,1,0:T(8,128)S(1)}, f32[5,3,1,8,128]{4,3,2,1,0:T(8,128)}, u32[]{:S(2)}) copy-start(f32[5,3,1,8,128]{4,3,2,1,0:T(8,128)} %param.4) | copy-start | bytes 184324
  231.6 5.6 %collective-permute-start.3 = (f32[9,1,10,1]{3,2,0,1:T(8,128)S(1)}, f32[9,1,10,1]{3,2,0,1:T(8,128)S(1)}, u32[]{:S(2)}, u32[]{:S(2)}) collective-permute-start(f32[9,1,10,1]{3,2,0,1:T(8,128)S(1)} %get-tuple-element.17), channel_id=1, source_target_pairs={{1,0},{2,1},{3,2},{4,3},{5,4},{6,5},{7,6},{9,8},{10,9},{11,10},{12... | collective-permute-start | bytes 1088 | tf_op jit(solution)/shard_map/ppermute | solution.py:19
  232.9 5.4 %collective-permute-start.2 = (f32[9,1,10,1]{3,2,0,1:T(8,128)S(1)}, f32[9,1,10,1]{3,2,0,1:T(8,128)S(1)}, u32[]{:S(2)}, u32[]{:S(2)}) collective-permute-start(f32[9,1,10,1]{3,2,0,1:T(8,128)S(1)} %get-tuple-element.16), channel_id=1, source_target_pairs={{0,1},{1,2},{2,3},{3,4},{4,5},{5,6},{6,7},{8,9},{9,10},{10,11},{11... | collective-permute-start | bytes 1088 | tf_op jit(solution)/shard_map/ppermute | solution.py:17
Sparse Core Ops, SparseCore 0:
  10.6 196.4 all-reduce.2
where the time goes:
time: 384 us
  waiting for transfers between devices  200 us (52%)
  blocking collectives  107 us (28%)
  between operations  39.1 us (10%)
  starting transfers between devices  28.2 us (7%)
  local copies, waits for them, and re-layouts  5.18 us (1%)
    psum x1, waiting for transfers between devices, per_device(): totals = lax.psum(partials[0], 'shot')  198 us
    psum x1, blocking collectives, per_device(): lax.psum((pair_dots(s_flat, y_flat), curv_part, hist_part, pre_part), ('s...  107 us
    ppermute x2, starting transfers between devices, extended_2(): lax.ppermute(head, axis, [((i + 1) % count, i) for i in range(ends)])  20 us
    ppermute x2, starting transfers between devices, extended_2(): lax.ppermute(tail, axis, [(i, (i + 1) % count) for i in range(ends)])  8.2 us
  transfers between devices with their start and end apart: 5, of which 3 were waited for; matrix products, arithmetic and copies ran while one was open for 0% of the time, Pallas kernels for 0%

commit v1 on v0

v1 whole, which is shorter than its diff:
```python
import jax
import jax.numpy as jnp
from jax import lax
from jax.experimental import pallas as pl
from jax.experimental.pallas import tpu as pltpu
from jax.sharding import PartitionSpec as P

PAIRS = 5
FIELDS = 9
Z = 12
X = 2
SHOT = Z * X
GX = 4
GY = 8
MESH = pl.DeviceIdType.MESH
SPLIT = 5

ORDER = (6, 5, -5, 4, -4, 3, -3, 2, -2, 1, -1, 0)
LAST = {3: 0, -3: 1, 2: 2, -2: 3, 1: 4, -1: 5}

CROSS = 0
CURV = 32
HIST = 47
PRE = 52
SUMS = 64


def rows_of(terms):
    sub = lax.broadcasted_iota(jnp.int32, (8, 128), 0)
    out = jnp.zeros((8, 128), jnp.float32)
    for i, term in enumerate(terms):
        out = jnp.where(sub == i, jnp.sum(term, axis=0, keepdims=True), out)
    return jnp.broadcast_to(jnp.sum(out, axis=1, keepdims=True), (8, 128))


def row_of_sums(terms, first):
    sub = lax.broadcasted_iota(jnp.int32, (8, 128), 0)
    lane = lax.broadcasted_iota(jnp.int32, (8, 128), 1)
    total = jnp.zeros((8, 128), jnp.float32)
    for start in range(0, len(terms), 8):
        tile = rows_of(terms[start : start + 8])
        total = total + jnp.where(lane == sub + (first + start), tile, 0.0)
    return jnp.sum(total, axis=0, keepdims=True)


def dot_tile(left, right):
    return left[0] * right[0] + left[1] * right[1] + left[2] * right[2]


def kernel(
    partials, hist_s, hist_y, out,
    own, pair, stage, last, s_tile, y_tile,
    rows_out, rows_in, cols_out, cols_in,
    row_a, all_a, row_b, all_b, splat,
    local_sem, pair_send, pair_recv, stage_send, stage_recv, last_send, last_recv,
    halo_send, halo_recv, a_send, a_recv, b_send, b_recv,
):
    shot = lax.axis_index("shot")
    gx = lax.axis_index("gx")
    gy = lax.axis_index("gy")
    z = lax.rem(shot, Z)
    xb = lax.div(shot, Z)
    base = xb * Z
    other = (1 - xb) * Z

    def along_z(step):
        return {"shot": base + lax.rem(z + (step + Z), Z)}

    def shot_peer(dx, dz):
        side = other if dx else base
        return {"shot": side + lax.rem(z + dz, Z)}

    def tile_peer(dx, dy):
        return {"gx": lax.rem(gx + (dx + GX), GX), "gy": lax.rem(gy + (dy + GY), GY)}

    shot_steps = [(dx, dz) for dx in range(X) for dz in range(Z) if (dx, dz) != (0, 0)]
    tile_steps = [(dx, dy) for dx in range(GX) for dy in range(GY) if (dx, dy) != (0, 0)]

    local = [
        pltpu.make_async_copy(partials.at[0, :, pl.ds(base, Z)], own, local_sem.at[0]),
        pltpu.make_async_copy(hist_s.at[:, :, 0], s_tile, local_sem.at[1]),
        pltpu.make_async_copy(hist_y.at[:, :, 0], y_tile, local_sem.at[2]),
    ]
    for copy in local:
        copy.start()

    barrier = pltpu.get_barrier_semaphore()
    for dx, dz in shot_steps:
        pl.semaphore_signal(barrier, inc=1, device_id=shot_peer(dx, dz), device_id_type=MESH)
    for dx, dy in tile_steps:
        pl.semaphore_signal(barrier, inc=1, device_id=tile_peer(dx, dy), device_id_type=MESH)
    pl.semaphore_wait(barrier, len(shot_steps) + len(tile_steps))

    started = []

    def send(src, dst, send_sem, recv_sem, device):
        copy = pltpu.make_async_remote_copy(
            src_ref=src, dst_ref=dst, send_sem=send_sem, recv_sem=recv_sem, device_id=device, device_id_type=MESH
        )
        copy.start()
        started.append(copy)
        return copy

    level = [lax.rem(z + (Z - s), Z) for s in ORDER]
    pair_copy = []
    for k in range(Z):
        pair_copy.append(
            send(partials.at[0, :, other + level[k]], pair.at[k], pair_send.at[k], pair_recv.at[k], {"shot": other + z})
        )

    local[1].wait()
    local[2].wait()
    s_vec = [[s_tile[i, c] for c in range(3)] for i in range(PAIRS)]
    y_vec = [[y_tile[i, c] for c in range(3)] for i in range(PAIRS)]
    cross = [dot_tile(s_vec[i], y_vec[j]) for i in range(PAIRS) for j in range(PAIRS)]
    row_a[0:1] = row_of_sums(cross, CROSS)
    local[0].wait()

    slot = {s: k for k, s in enumerate(ORDER)}
    stage_copy = {}
    last_copy = {}
    for s in (6, 5, -5, 4, -4):
        k = slot[s]
        pair_copy[k].wait_recv()
        pair[k] = pair[k] + own[:, level[k]]
        if s == 6:
            stage_copy["r6"] = send(
                pair.at[k, 0:SPLIT], stage.at[2, 0:SPLIT], stage_send.at[2], stage_recv.at[2], along_z(-3)
            )
            stage_copy["l6"] = send(
                pair.at[k, SPLIT:FIELDS], stage.at[5, SPLIT:FIELDS], stage_send.at[5], stage_recv.at[5], along_z(3)
            )
        elif s > 0:
            stage_copy[s] = send(pair.at[k], stage.at[s - 4], stage_send.at[s - 4], stage_recv.at[s - 4], along_z(3 - s))
        else:
            stage_copy[s] = send(
                pair.at[k], stage.at[-s - 1], stage_send.at[-s - 1], stage_recv.at[-s - 1], along_z(-3 - s)
            )
    for s in (3, -3, 2, -2, 1, -1):
        k = slot[s]
        pair_copy[k].wait_recv()
        pair[k] = pair[k] + own[:, level[k]]
        if abs(s) < 3:
            m = LAST[s]
            last_copy[s] = send(pair.at[k], last.at[m], last_send.at[m], last_recv.at[m], along_z(-s))
    for s in (3, -3):
        k = slot[s]
        m = LAST[s]
        if s > 0:
            stage_copy["r6"].wait_recv()
            stage_copy[5].wait_recv()
            stage_copy[4].wait_recv()
            pair[k] = pair[k] + stage[0] + stage[1]
            pair[k, 0:SPLIT] = pair[k, 0:SPLIT] + stage[2, 0:SPLIT]
        else:
            stage_copy["l6"].wait_recv()
            stage_copy[-5].wait_recv()
            stage_copy[-4].wait_recv()
            pair[k] = pair[k] + stage[3] + stage[4]
            pair[k, SPLIT:FIELDS] = pair[k, SPLIT:FIELDS] + stage[5, SPLIT:FIELDS]
        last_copy[s] = send(pair.at[k], last.at[m], last_send.at[m], last_recv.at[m], along_z(-s))
    k = slot[0]
    pair_copy[k].wait_recv()
    mine = pair[k] + own[:, z]
    for s in (1, -1, 2, -2, 3, -3):
        last_copy[s].wait_recv()
        mine = mine + last[LAST[s]]
    mine = mine * (1.0 / SHOT)
    field = [mine[f] for f in range(FIELDS)]

    sub = lax.broadcasted_iota(jnp.int32, (8, 128), 0)
    lane = lax.broadcasted_iota(jnp.int32, (8, 128), 1)
    columns = jnp.zeros((8, 128), jnp.float32)
    for f in range(FIELDS):
        rows_out[0, f : f + 1] = field[f][0:1]
        rows_out[1, f : f + 1] = field[f][7:8]
        columns = jnp.where(lane == f, field[f] if f == 0 else pltpu.roll(field[f], f, 1), columns)
        columns = jnp.where(lane == 16 + f, pltpu.roll(field[f], 17 + f, 1), columns)
    cols_out[...] = columns
    halo = []
    for n, (dx, dy) in enumerate(((-1, -1), (1, -1), (-1, 1), (1, 1), (0, -1), (0, 1))):
        halo.append(send(cols_out, cols_in.at[n], halo_send.at[n], halo_recv.at[n], tile_peer(dx, dy)))
    halo.append(send(rows_out.at[0, 0:FIELDS], rows_in.at[0, 0:FIELDS], halo_send.at[6], halo_recv.at[6], tile_peer(-1, 0)))
    halo.append(send(rows_out.at[1, 0:FIELDS], rows_in.at[1, 0:FIELDS], halo_send.at[7], halo_recv.at[7], tile_peer(1, 0)))
    for copy in halo:
        copy.wait_recv()
    has_up, has_down = gx > 0, gx < GX - 1
    has_left, has_right = gy > 0, gy < GY - 1

    def along_x(center, above, below):
        up = jnp.where(sub == 0, jnp.where(has_up, above, 0.0), pltpu.roll(center, 1, 0))
        down = jnp.where(sub == 7, jnp.where(has_down, below, 0.0), pltpu.roll(center, 7, 0))
        return 0.25 * (up + 2.0 * center + down)

    def wide(row):
        return jnp.broadcast_to(row, (8, 128))

    left = along_x(cols_in[5], wide(cols_in[3, 7:8]), wide(cols_in[2, 0:1]))
    right = along_x(cols_in[4], wide(cols_in[1, 7:8]), wide(cols_in[0, 0:1]))
    left = jnp.where(has_left, left, 0.0)
    right = jnp.where(has_right, right, 0.0)
    smooth = []
    for f in range(FIELDS):
        mid = along_x(field[f], wide(rows_in[1, f : f + 1]), wide(rows_in[0, f : f + 1]))
        before = jnp.where(lane == 0, pltpu.roll(left, 112 - f, 1), pltpu.roll(mid, 1, 1))
        after = jnp.where(lane == 127, pltpu.roll(right, 127 - f, 1), pltpu.roll(mid, 127, 1))
        smooth.append(0.25 * (before + 2.0 * mid + after))

    gradient = smooth[0:3]
    diag_p, diag_s, diag_r, cross_ps, cross_pr, cross_sr = smooth[3:9]
    cof_pp = diag_s * diag_r - cross_sr * cross_sr
    cof_ps = cross_pr * cross_sr - cross_ps * diag_r
    cof_pr = cross_ps * cross_sr - diag_s * cross_pr
    cof_ss = diag_p * diag_r - cross_pr * cross_pr
    cof_sr = cross_ps * cross_pr - diag_p * cross_sr
    cof_rr = diag_p * diag_s - cross_ps * cross_ps
    inverse_det = 1.0 / (diag_p * cof_pp + cross_ps * cof_ps + cross_pr * cof_pr)

    def solve(v):
        return [
            (cof_pp * v[0] + cof_ps * v[1] + cof_pr * v[2]) * inverse_det,
            (cof_ps * v[0] + cof_ss * v[1] + cof_sr * v[2]) * inverse_det,
            (cof_pr * v[0] + cof_sr * v[1] + cof_rr * v[2]) * inverse_det,
        ]

    first = solve(gradient)
    solved = [solve(y_vec[i]) for i in range(PAIRS)]
    upper = [(i, j) for i in range(PAIRS) for j in range(i, PAIRS)]
    terms = [dot_tile(y_vec[i], solved[j]) for i, j in upper]
    terms += [dot_tile(s_vec[i], gradient) for i in range(PAIRS)]
    terms += [dot_tile(y_vec[i], first) for i in range(PAIRS)]
    row = row_a[0:1] + row_of_sums(terms, CURV)

    row_a[0:1] = row
    all_a[0:1] = row
    for n, (dx, dz) in enumerate(shot_steps):
        send(row_a.at[0:1], all_a.at[n + 1 : n + 2], a_send, a_recv, shot_peer(dx, dz))
        started.pop()
    rest_a = all_a.at[1:SHOT]
    pltpu.make_async_copy(rest_a, rest_a, a_recv).wait()
    row = jnp.sum(all_a[...], axis=0, keepdims=True)
    row_b[0:1] = row
    all_b[0:1] = row
    for n, (dx, dy) in enumerate(tile_steps):
        send(row_b.at[0:1], all_b.at[n + 1 : n + 2], b_send, b_recv, tile_peer(dx, dy))
        started.pop()
    rest_b = all_b.at[1 : GX * GY]
    pltpu.make_async_copy(rest_b, rest_b, b_recv).wait()
    row = jnp.sum(all_b[...], axis=0, keepdims=True)

    tall_row = lax.broadcasted_iota(jnp.int32, (SUMS, 128), 0)
    tall_lane = lax.broadcasted_iota(jnp.int32, (SUMS, 128), 1)
    picked = jnp.where(tall_row == tall_lane, jnp.broadcast_to(row, (SUMS, 128)), 0.0)
    splat[...] = jnp.broadcast_to(jnp.sum(picked, axis=1, keepdims=True), (SUMS, 128))

    def total(n):
        return splat[n : n + 1]

    cross_gram = [[total(CROSS + i * PAIRS + j) for j in range(PAIRS)] for i in range(PAIRS)]
    curv_gram = [[None] * PAIRS for _ in range(PAIRS)]
    for n, (i, j) in enumerate(upper):
        curv_gram[i][j] = curv_gram[j][i] = total(CURV + n)
    coef_p = [None] * PAIRS
    for i in range(PAIRS - 1, -1, -1):
        value = total(HIST + i)
        for j in range(i + 1, PAIRS):
            value = value - cross_gram[i][j] * coef_p[j]
        coef_p[i] = value / cross_gram[i][i]
    coef_q = [None] * PAIRS
    for i in range(PAIRS):
        value = cross_gram[i][i] * coef_p[i] - total(PRE + i)
        for j in range(PAIRS):
            value = value + curv_gram[i][j] * coef_p[j]
        for j in range(i):
            value = value - cross_gram[j][i] * coef_q[j]
        coef_q[i] = value / cross_gram[i][i]
    for c in range(3):
        value = first[c]
        for i in range(PAIRS):
            value = value + wide(coef_q[i]) * s_vec[i][c] - wide(coef_p[i]) * solved[i][c]
        out[c, 0] = -value

    for copy in started:
        copy.wait_send()
    pltpu.make_async_copy(rest_a, rest_a, a_send).wait()
    pltpu.make_async_copy(rest_b, rest_b, b_send).wait()


def per_device(partials, hist_s, hist_y):
    dma = pltpu.SemaphoreType.DMA
    f32 = jnp.float32
    chunk = (FIELDS, 8, 128)
    return pl.pallas_call(
        kernel,
        out_shape=jax.ShapeDtypeStruct((3, 1, 8, 128), f32),
        in_specs=[pl.BlockSpec(memory_space=pl.ANY)] * 3,
        out_specs=pl.BlockSpec(memory_space=pltpu.VMEM),
        scratch_shapes=[
            pltpu.VMEM((FIELDS, Z, 8, 128), f32),
            pltpu.VMEM((Z, *chunk), f32),
            pltpu.VMEM((6, *chunk), f32),
            pltpu.VMEM((6, *chunk), f32),
            pltpu.VMEM((PAIRS, 3, 8, 128), f32),
            pltpu.VMEM((PAIRS, 3, 8, 128), f32),
            pltpu.VMEM((2, 16, 128), f32),
            pltpu.VMEM((2, 16, 128), f32),
            pltpu.VMEM((8, 128), f32),
            pltpu.VMEM((6, 8, 128), f32),
            pltpu.VMEM((8, 128), f32),
            pltpu.VMEM((SHOT, 128), f32),
            pltpu.VMEM((8, 128), f32),
            pltpu.VMEM((GX * GY, 128), f32),
            pltpu.VMEM((SUMS, 128), f32),
            dma((3,)),
            dma((Z,)), dma((Z,)),
            dma((6,)), dma((6,)),
            dma((6,)), dma((6,)),
            dma((8,)), dma((8,)),
            dma, dma, dma, dma,
        ],
        compiler_params=pltpu.CompilerParams(collective_id=0, has_side_effects=True),
        name="lbfgs_direction",
    )(partials, hist_s, hist_y)


def solution(mesh):
    return jax.shard_map(
        per_device,
        mesh=mesh,
        in_specs=(
            P("shot", None, None, "gx", "gy"),
            P(None, None, "shot", "gx", "gy"),
            P(None, None, "shot", "gx", "gy"),
        ),
        out_specs=P(None, "shot", "gx", "gy"),
        check_vma=False,
    )
```

time: 384 us -> 55.5 us (0.14)
  waiting for transfers between devices: 200 us -> 0 us
  blocking collectives: 107 us -> 0 us
  Pallas kernels: 0 us -> 54 us
  between operations: 39.1 us -> 0.01 us
  starting transfers between devices: 28.2 us -> 0 us
  local copies, waits for them, and re-layouts: 5.18 us -> 1.31 us
    psum x1 -> x0, waiting for transfers between devices: 198 us -> none  [per_device(): totals = lax.psum(partials[0], 'shot')]
    psum x1 -> x0, blocking collectives: 107 us -> none  [per_device(): lax.psum((pair_dots(s_flat, y_flat), curv_part, hist_part, pre_part), ('s...]
    pallas_call x0 -> x1, Pallas kernels: none -> 54 us  [per_device(): pl.pallas_call(kernel, out_shape=jax.ShapeDtypeStruct((3, 1, 8, 128), f32...]
    ppermute x4 -> x0, starting transfers between devices: 28.2 us -> none  [the longest x2 20 us: extended_2(): lax.ppermute(head, axis, [((i + 1) % count, i) for i in range(ends)])]
  transfers between devices with their start and end apart: 5 -> 0, of which waited for: 3 -> 0; matrix products, arithmetic and copies ran while one was open for 0% -> 0% of each run, Pallas kernels for 0% -> 0%
where the time goes in v1:
time: 55.5 us; the launch traced here: 55.3 us
  Pallas kernels  54 us (97%)
  local copies, waits for them, and re-layouts  1.31 us (2%)
    pallas_call x1, Pallas kernels, per_device(): pl.pallas_call(kernel, out_shape=jax.ShapeDtypeStruct((3, 1, 8, 128), f32...  54 us
    unnamed x1, local copies, waits for them, and re-layouts  1.31 us

profile of v1, /device:TPU:1, one launch (start us, length us, event | category | flops | bytes accessed | tf_op | source)
XLA Modules:
  0.0 55.3 jit_solution(7072045113902478801)
XLA Ops:
  0.0 54.0 %lbfgs_direction.1 = f32[3,1,8,128]{3,2,1,0:T(8,128)} custom-call(f32[1,9,24,8,128]{4,3,2,1,0:T(8,128)} %partials.1, f32[5,3,1,8,128]{4,3,2,1,0:T(8,128)} %hist_s.1, f32[5,3,1,8,128]{4,3,2,1,0:T(8,128)} %hist_y.1), custom_call_target="tpu_custom_call" | custom-call | tf_op jit(solution)/shard_map/lbfgs_direction/pallas_call | solution.py:293
  54.0 1.3 %copy.5 = f32[3,1,8,128]{3,2,1,0:T(8,128)} copy(f32[3,1,8,128]{3,2,1,0:T(8,128)} %lbfgs_direction.1) | data formatting | bytes 24576

commit v2 on v1

--- a/solution.py
+++ b/solution.py
@@ -16,6 +16,7 @@
 SPLIT = 5
 
 ORDER = (6, 5, -5, 4, -4, 3, -3, 2, -2, 1, -1, 0)
+STEPS = (1, 2, 3, -1, -2, -3)
 LAST = {3: 0, -3: 1, 2: 2, -2: 3, 1: 4, -1: 5}
 
 CROSS = 0
@@ -53,7 +54,7 @@
     rows_out, rows_in, cols_out, cols_in,
     row_a, all_a, row_b, all_b, splat,
     local_sem, pair_send, pair_recv, stage_send, stage_recv, last_send, last_recv,
-    halo_send, halo_recv, a_send, a_recv, b_send, b_recv,
+    halo_send, halo_recv, a_send, a_recv, b_send, b_recv, ready, known,
 ):
     shot = lax.axis_index("shot")
     gx = lax.axis_index("gx")
@@ -74,7 +75,9 @@
         return {"gx": lax.rem(gx + (dx + GX), GX), "gy": lax.rem(gy + (dy + GY), GY)}
 
     shot_steps = [(dx, dz) for dx in range(X) for dz in range(Z) if (dx, dz) != (0, 0)]
+    shot_steps.sort(key=lambda d: -(d[0] + min(d[1], Z - d[1])))
     tile_steps = [(dx, dy) for dx in range(GX) for dy in range(GY) if (dx, dy) != (0, 0)]
+    tile_steps.sort(key=lambda d: -(min(d[0], 2) + min(d[1], GY - d[1])))
 
     local = [
         pltpu.make_async_copy(partials.at[0, :, pl.ds(base, Z)], own, local_sem.at[0]),
@@ -84,12 +87,46 @@
     for copy in local:
         copy.start()
 
+    def plane(step):
+        return lax.rem(z + (step + Z), Z)
+
+    flip = lax.rem(gx + 2, GX)
+    mate = gx + 1 - 2 * lax.rem(gx, 2)
+    beside = (
+        {"shot": other + z},
+        {"shot": other + z, "gx": flip},
+        {"gx": mate},
+        tile_peer(0, 1),
+        tile_peer(0, -1),
+    )
     barrier = pltpu.get_barrier_semaphore()
-    for dx, dz in shot_steps:
-        pl.semaphore_signal(barrier, inc=1, device_id=shot_peer(dx, dz), device_id_type=MESH)
-    for dx, dy in tile_steps:
-        pl.semaphore_signal(barrier, inc=1, device_id=tile_peer(dx, dy), device_id_type=MESH)
-    pl.semaphore_wait(barrier, len(shot_steps) + len(tile_steps))
+
+    def signal(sem, device):
+        pl.semaphore_signal(sem, inc=1, device_id=device, device_id_type=MESH)
+
+    for device in beside:
+        signal(barrier, device)
+    lower = 0
+    for step in STEPS:
+
+        @pl.when(plane(step) > z)
+        def _(step=step):
+            signal(barrier, along_z(step))
+
+        lower = lower + jnp.where(plane(step) < z, 1, 0)
+    pl.semaphore_wait(barrier, len(beside) + lower)
+    for step in STEPS:
+
+        @pl.when(plane(step) < z)
+        def _(step=step):
+            signal(ready.at[STEPS.index(-step)], along_z(step))
+
+    def await_plane(step):
+        @pl.when(plane(step) > z)
+        def _():
+            pl.semaphore_wait(ready.at[STEPS.index(step)], 1)
+
+    signal(known.at[0], {"shot": other + z})
 
     started = []
 
@@ -115,6 +152,20 @@
     cross = [dot_tile(s_vec[i], y_vec[j]) for i in range(PAIRS) for j in range(PAIRS)]
     row_a[0:1] = row_of_sums(cross, CROSS)
     local[0].wait()
+
+    pl.semaphore_wait(known.at[0], 1)
+    signal(known.at[1], {"gx": mate})
+    pl.semaphore_wait(known.at[1], 1)
+
+    def pass_on(distance):
+        if distance > 1:
+            pl.semaphore_wait(known.at[2 * distance - 2], 1)
+            pl.semaphore_wait(known.at[2 * distance - 1], 1)
+        if distance <= GY // 2:
+            signal(known.at[2 * distance], tile_peer(0, 1))
+            signal(known.at[2 * distance + 1], tile_peer(0, -1))
+
+    pass_on(1)
 
     slot = {s: k for k, s in enumerate(ORDER)}
     stage_copy = {}
@@ -124,6 +175,8 @@
         pair_copy[k].wait_recv()
         pair[k] = pair[k] + own[:, level[k]]
         if s == 6:
+            await_plane(-3)
+            await_plane(3)
             stage_copy["r6"] = send(
                 pair.at[k, 0:SPLIT], stage.at[2, 0:SPLIT], stage_send.at[2], stage_recv.at[2], along_z(-3)
             )
@@ -131,12 +184,19 @@
                 pair.at[k, SPLIT:FIELDS], stage.at[5, SPLIT:FIELDS], stage_send.at[5], stage_recv.at[5], along_z(3)
             )
         elif s > 0:
+            await_plane(3 - s)
             stage_copy[s] = send(pair.at[k], stage.at[s - 4], stage_send.at[s - 4], stage_recv.at[s - 4], along_z(3 - s))
         else:
+            await_plane(-3 - s)
             stage_copy[s] = send(
                 pair.at[k], stage.at[-s - 1], stage_send.at[-s - 1], stage_recv.at[-s - 1], along_z(-3 - s)
             )
+    pass_on(2)
     for s in (3, -3, 2, -2, 1, -1):
+        if s == -3:
+            pass_on(3)
+        if s == -2:
+            pass_on(4)
         k = slot[s]
         pair_copy[k].wait_recv()
         pair[k] = pair[k] + own[:, level[k]]
@@ -159,6 +219,7 @@
             pair[k] = pair[k] + stage[3] + stage[4]
             pair[k, SPLIT:FIELDS] = pair[k, SPLIT:FIELDS] + stage[5, SPLIT:FIELDS]
         last_copy[s] = send(pair.at[k], last.at[m], last_send.at[m], last_recv.at[m], along_z(-s))
+    pass_on(5)
     k = slot[0]
     pair_copy[k].wait_recv()
     mine = pair[k] + own[:, z]
@@ -293,7 +354,7 @@
     return pl.pallas_call(
         kernel,
         out_shape=jax.ShapeDtypeStruct((3, 1, 8, 128), f32),
-        in_specs=[pl.BlockSpec(memory_space=pl.ANY)] * 3,
+        in_specs=[pl.BlockSpec(memory_space=pltpu.HBM)] * 3,
         out_specs=pl.BlockSpec(memory_space=pltpu.VMEM),
         scratch_shapes=[
             pltpu.VMEM((FIELDS, Z, 8, 128), f32),
@@ -317,8 +378,10 @@
             dma((6,)), dma((6,)),
             dma((8,)), dma((8,)),
             dma, dma, dma, dma,
+            pltpu.SemaphoreType.REGULAR((len(STEPS),)),
+            pltpu.SemaphoreType.REGULAR((2 + GY,)),
         ],
-        compiler_params=pltpu.CompilerParams(collective_id=0, has_side_effects=True),
+        compiler_params=pltpu.CompilerParams(collective_id=0, has_side_effects=True, vmem_limit_bytes=56_512_000),
         name="lbfgs_direction",
     )(partials, hist_s, hist_y)
 

time: 55.5 us -> 50.6 us (0.912)
  Pallas kernels: 54 us -> 49.9 us
  local copies, waits for them, and re-layouts: 1.31 us -> 0.6 us
    pallas_call x1, Pallas kernels: 54 us -> 49.9 us  [per_device(): pl.pallas_call(kernel, out_shape=jax.ShapeDtypeStruct((3, 1, 8, 128), f32...]
    unnamed x1, local copies, waits for them, and re-layouts: 1.31 us -> 0.6 us
where the time goes in v2:
time: 50.6 us; the launch traced here: 50.5 us
  Pallas kernels  49.9 us (99%)
  local copies, waits for them, and re-layouts  0.6 us (1%)
    pallas_call x1, Pallas kernels, per_device(): pl.pallas_call(kernel, out_shape=jax.ShapeDtypeStruct((3, 1, 8, 128), f32...  49.9 us

profile of v2, /device:TPU:1, one launch (start us, length us, event | category | flops | bytes accessed | tf_op | source)
XLA Modules:
  0.0 50.5 jit_solution(12472789602527146327)
XLA Ops:
  0.0 49.9 %lbfgs_direction.1 = f32[3,1,8,128]{3,2,1,0:T(8,128)S(1)} custom-call(f32[1,9,24,8,128]{4,3,2,1,0:T(8,128)} %partials.1, f32[5,3,1,8,128]{4,3,2,1,0:T(8,128)} %hist_s.1, f32[5,3,1,8,128]{4,3,2,1,0:T(8,128)} %hist_y.1), custom_call_target="tpu_custom_call" | custom-call | tf_op jit(solution)/shard_map/lbfgs_direction/pallas_call | solution.py:354
  49.9 0.6 %copy.5 = f32[3,1,8,128]{3,2,1,0:T(8,128)} copy(f32[3,1,8,128]{3,2,1,0:T(8,128)S(1)} %lbfgs_direction.1) | data formatting | bytes 24576

commit v3 on v1

--- a/solution.py
+++ b/solution.py
@@ -16,6 +16,7 @@
 SPLIT = 5
 
 ORDER = (6, 5, -5, 4, -4, 3, -3, 2, -2, 1, -1, 0)
+STEPS = (1, 2, 3, -1, -2, -3)
 LAST = {3: 0, -3: 1, 2: 2, -2: 3, 1: 4, -1: 5}
 
 CROSS = 0
@@ -53,7 +54,7 @@
     rows_out, rows_in, cols_out, cols_in,
     row_a, all_a, row_b, all_b, splat,
     local_sem, pair_send, pair_recv, stage_send, stage_recv, last_send, last_recv,
-    halo_send, halo_recv, a_send, a_recv, b_send, b_recv,
+    halo_send, halo_recv, a_send, a_recv, b_send, b_recv, ready, known,
 ):
     shot = lax.axis_index("shot")
     gx = lax.axis_index("gx")
@@ -74,22 +75,91 @@
         return {"gx": lax.rem(gx + (dx + GX), GX), "gy": lax.rem(gy + (dy + GY), GY)}
 
     shot_steps = [(dx, dz) for dx in range(X) for dz in range(Z) if (dx, dz) != (0, 0)]
+    shot_steps.sort(key=lambda d: -(d[0] + min(d[1], Z - d[1])))
     tile_steps = [(dx, dy) for dx in range(GX) for dy in range(GY) if (dx, dy) != (0, 0)]
+    tile_steps.sort(key=lambda d: -(min(d[0], 2) + min(d[1], GY - d[1])))
 
     local = [
-        pltpu.make_async_copy(partials.at[0, :, pl.ds(base, Z)], own, local_sem.at[0]),
+        pltpu.make_async_copy(partials.at[0], own, local_sem.at[0]),
         pltpu.make_async_copy(hist_s.at[:, :, 0], s_tile, local_sem.at[1]),
         pltpu.make_async_copy(hist_y.at[:, :, 0], y_tile, local_sem.at[2]),
     ]
     for copy in local:
         copy.start()
 
+    def plane(step):
+        return lax.rem(z + (step + Z), Z)
+
+    half = GY // 2
+    ring = jnp.where(gy > half, GY - gy, gy)
+    flip = {"gx": lax.rem(gx + 2, GX)}
+    mate = {"gx": gx + 1 - 2 * lax.rem(gx, 2)}
+    outer = [(tile_peer(0, 1), gy < half), (tile_peer(0, -1), (gy == 0) | (gy > half))]
+    inner = [(tile_peer(0, -1), (gy > 0) & (gy <= half)), (tile_peer(0, 1), gy >= half)]
     barrier = pltpu.get_barrier_semaphore()
-    for dx, dz in shot_steps:
-        pl.semaphore_signal(barrier, inc=1, device_id=shot_peer(dx, dz), device_id_type=MESH)
-    for dx, dy in tile_steps:
-        pl.semaphore_signal(barrier, inc=1, device_id=tile_peer(dx, dy), device_id_type=MESH)
-    pl.semaphore_wait(barrier, len(shot_steps) + len(tile_steps))
+
+    def signal(sem, device):
+        pl.semaphore_signal(sem, inc=1, device_id=device, device_id_type=MESH)
+
+    def signal_if(wanted, sem, device):
+        @pl.when(wanted)
+        def _():
+            signal(sem, device)
+
+    signal(barrier, {"shot": other + z})
+    signal(barrier, mate)
+    expected = 2 + jnp.where(gx >= 2, 1, 0) + jnp.where(gy == half, 2, jnp.where(gy == 0, 0, 1))
+    for device, wanted in outer:
+        signal_if(wanted, barrier, device)
+    signal_if(gx < 2, barrier, flip)
+    for step in STEPS:
+        signal_if(plane(step) > z, barrier, along_z(step))
+        expected = expected + jnp.where(plane(step) < z, 1, 0)
+    pl.semaphore_wait(barrier, expected)
+
+    def tell_earlier():
+        for step in STEPS:
+            signal_if(plane(step) < z, ready.at[STEPS.index(-step)], along_z(step))
+        signal_if(gx >= 2, known.at[0], flip)
+
+    def await_plane(step):
+        @pl.when(plane(step) > z)
+        def _():
+            pl.semaphore_wait(ready.at[STEPS.index(step)], 1)
+
+    def know_row():
+        @pl.when(gx < 2)
+        def _():
+            pl.semaphore_wait(known.at[0], 1)
+
+        signal(known.at[1], mate)
+        pl.semaphore_wait(known.at[1], 1)
+
+        @pl.when(ring == half)
+        def _():
+            for device, _ in inner:
+                signal(known.at[2], device)
+
+    def know_outer(distance):
+        @pl.when(ring == distance)
+        def _():
+            pl.semaphore_wait(known.at[2], 1 if distance else 2)
+            if distance:
+                for device, wanted in inner:
+                    signal_if(wanted, known.at[2], device)
+            else:
+                for device, _ in outer:
+                    signal(known.at[3], device)
+
+    def know_all():
+        @pl.when(ring > 0)
+        def _():
+            pl.semaphore_wait(known.at[3], jnp.where(ring == half, 2, 1))
+
+            @pl.when(ring < half)
+            def _():
+                for device, wanted in outer:
+                    signal_if(wanted, known.at[3], device)
 
     started = []
 
@@ -101,29 +171,37 @@
         started.append(copy)
         return copy
 
+    local[0].wait()
     level = [lax.rem(z + (Z - s), Z) for s in ORDER]
     pair_copy = []
     for k in range(Z):
         pair_copy.append(
-            send(partials.at[0, :, other + level[k]], pair.at[k], pair_send.at[k], pair_recv.at[k], {"shot": other + z})
+            send(own.at[:, other + level[k]], pair.at[k], pair_send.at[k], pair_recv.at[k], {"shot": other + z})
         )
 
+    tell_earlier()
     local[1].wait()
     local[2].wait()
     s_vec = [[s_tile[i, c] for c in range(3)] for i in range(PAIRS)]
     y_vec = [[y_tile[i, c] for c in range(3)] for i in range(PAIRS)]
     cross = [dot_tile(s_vec[i], y_vec[j]) for i in range(PAIRS) for j in range(PAIRS)]
     row_a[0:1] = row_of_sums(cross, CROSS)
-    local[0].wait()
-
+
+    know_row()
     slot = {s: k for k, s in enumerate(ORDER)}
     stage_copy = {}
     last_copy = {}
     for s in (6, 5, -5, 4, -4):
         k = slot[s]
         pair_copy[k].wait_recv()
-        pair[k] = pair[k] + own[:, level[k]]
+        pair[k] = pair[k] + own[:, base + level[k]]
+        if s == 5:
+            know_outer(3)
+        if s == 4:
+            know_outer(2)
         if s == 6:
+            await_plane(-3)
+            await_plane(3)
             stage_copy["r6"] = send(
                 pair.at[k, 0:SPLIT], stage.at[2, 0:SPLIT], stage_send.at[2], stage_recv.at[2], along_z(-3)
             )
@@ -131,37 +209,51 @@
                 pair.at[k, SPLIT:FIELDS], stage.at[5, SPLIT:FIELDS], stage_send.at[5], stage_recv.at[5], along_z(3)
             )
         elif s > 0:
+            await_plane(3 - s)
             stage_copy[s] = send(pair.at[k], stage.at[s - 4], stage_send.at[s - 4], stage_recv.at[s - 4], along_z(3 - s))
         else:
+            await_plane(-3 - s)
             stage_copy[s] = send(
                 pair.at[k], stage.at[-s - 1], stage_send.at[-s - 1], stage_recv.at[-s - 1], along_z(-3 - s)
             )
-    for s in (3, -3, 2, -2, 1, -1):
+    def add_own(s):
         k = slot[s]
         pair_copy[k].wait_recv()
-        pair[k] = pair[k] + own[:, level[k]]
-        if abs(s) < 3:
-            m = LAST[s]
-            last_copy[s] = send(pair.at[k], last.at[m], last_send.at[m], last_recv.at[m], along_z(-s))
-    for s in (3, -3):
+        pair[k] = pair[k] + own[:, base + level[k]]
+
+    def send_last(s):
+        m = LAST[s]
+        last_copy[s] = send(pair.at[slot[s]], last.at[m], last_send.at[m], last_recv.at[m], along_z(-s))
+
+    def gather(s):
         k = slot[s]
-        m = LAST[s]
         if s > 0:
-            stage_copy["r6"].wait_recv()
-            stage_copy[5].wait_recv()
-            stage_copy[4].wait_recv()
-            pair[k] = pair[k] + stage[0] + stage[1]
-            pair[k, 0:SPLIT] = pair[k, 0:SPLIT] + stage[2, 0:SPLIT]
+            first_slot, low, high, far = 0, 0, SPLIT, "r6"
         else:
-            stage_copy["l6"].wait_recv()
-            stage_copy[-5].wait_recv()
-            stage_copy[-4].wait_recv()
-            pair[k] = pair[k] + stage[3] + stage[4]
-            pair[k, SPLIT:FIELDS] = pair[k, SPLIT:FIELDS] + stage[5, SPLIT:FIELDS]
-        last_copy[s] = send(pair.at[k], last.at[m], last_send.at[m], last_recv.at[m], along_z(-s))
+            first_slot, low, high, far = 3, SPLIT, FIELDS, "l6"
+        add_own(s)
+        for key in (far, s + s // 3 * 2, s + s // 3):
+            stage_copy[key].wait_recv()
+        pair[k] = pair[k] + stage[first_slot] + stage[first_slot + 1]
+        pair[k, low:high] = pair[k, low:high] + stage[first_slot + 2, low:high]
+        send_last(s)
+
+    add_own(2)
+    send_last(2)
+    know_outer(1)
+    add_own(-2)
+    send_last(-2)
+    gather(3)
+    gather(-3)
+    know_outer(0)
+    add_own(1)
+    send_last(1)
+    add_own(-1)
+    send_last(-1)
+    know_all()
     k = slot[0]
     pair_copy[k].wait_recv()
-    mine = pair[k] + own[:, z]
+    mine = pair[k] + own[:, shot]
     for s in (1, -1, 2, -2, 3, -3):
         last_copy[s].wait_recv()
         mine = mine + last[LAST[s]]
@@ -293,10 +385,10 @@
     return pl.pallas_call(
         kernel,
         out_shape=jax.ShapeDtypeStruct((3, 1, 8, 128), f32),
-        in_specs=[pl.BlockSpec(memory_space=pl.ANY)] * 3,
+        in_specs=[pl.BlockSpec(memory_space=pltpu.HBM)] * 3,
         out_specs=pl.BlockSpec(memory_space=pltpu.VMEM),
         scratch_shapes=[
-            pltpu.VMEM((FIELDS, Z, 8, 128), f32),
+            pltpu.VMEM((FIELDS, SHOT, 8, 128), f32),
             pltpu.VMEM((Z, *chunk), f32),
             pltpu.VMEM((6, *chunk), f32),
             pltpu.VMEM((6, *chunk), f32),
@@ -317,8 +409,10 @@
             dma((6,)), dma((6,)),
             dma((8,)), dma((8,)),
             dma, dma, dma, dma,
+            pltpu.SemaphoreType.REGULAR((len(STEPS),)),
+            pltpu.SemaphoreType.REGULAR((4,)),
         ],
-        compiler_params=pltpu.CompilerParams(collective_id=0, has_side_effects=True),
+        compiler_params=pltpu.CompilerParams(collective_id=0, has_side_effects=True, vmem_limit_bytes=56_512_000),
         name="lbfgs_direction",
     )(partials, hist_s, hist_y)
 

time: 55.5 us -> 49.3 us (0.89)
  Pallas kernels: 54 us -> 48.6 us
  local copies, waits for them, and re-layouts: 1.31 us -> 0.6 us
    pallas_call x1, Pallas kernels: 54 us -> 48.6 us  [per_device(): pl.pallas_call(kernel, out_shape=jax.ShapeDtypeStruct((3, 1, 8, 128), f32...]
    unnamed x1, local copies, waits for them, and re-layouts: 1.31 us -> 0.6 us
where the time goes in v3:
time: 49.3 us; the launch traced here: 49.2 us
  Pallas kernels  48.6 us (99%)
  local copies, waits for them, and re-layouts  0.6 us (1%)
    pallas_call x1, Pallas kernels, per_device(): pl.pallas_call(kernel, out_shape=jax.ShapeDtypeStruct((3, 1, 8, 128), f32...  48.6 us

profile of v3, /device:TPU:1, one launch (start us, length us, event | category | flops | bytes accessed | tf_op | source)
XLA Modules:
  0.0 49.2 jit_solution(16665982697933243769)
XLA Ops:
  0.0 48.6 %lbfgs_direction.1 = f32[3,1,8,128]{3,2,1,0:T(8,128)S(1)} custom-call(f32[1,9,24,8,128]{4,3,2,1,0:T(8,128)} %partials.1, f32[5,3,1,8,128]{4,3,2,1,0:T(8,128)} %hist_s.1, f32[5,3,1,8,128]{4,3,2,1,0:T(8,128)} %hist_y.1), custom_call_target="tpu_custom_call" | custom-call | tf_op jit(solution)/shard_map/lbfgs_direction/pallas_call | solution.py:385
  48.6 0.6 %copy.5 = f32[3,1,8,128]{3,2,1,0:T(8,128)} copy(f32[3,1,8,128]{3,2,1,0:T(8,128)S(1)} %lbfgs_direction.1) | data formatting | bytes 24576

commit v4 on v3

--- a/solution.py
+++ b/solution.py
@@ -67,17 +67,16 @@
     def along_z(step):
         return {"shot": base + lax.rem(z + (step + Z), Z)}
 
-    def shot_peer(dx, dz):
-        side = other if dx else base
-        return {"shot": side + lax.rem(z + dz, Z)}
-
     def tile_peer(dx, dy):
         return {"gx": lax.rem(gx + (dx + GX), GX), "gy": lax.rem(gy + (dy + GY), GY)}
 
-    shot_steps = [(dx, dz) for dx in range(X) for dz in range(Z) if (dx, dz) != (0, 0)]
-    shot_steps.sort(key=lambda d: -(d[0] + min(d[1], Z - d[1])))
-    tile_steps = [(dx, dy) for dx in range(GX) for dy in range(GY) if (dx, dy) != (0, 0)]
-    tile_steps.sort(key=lambda d: -(min(d[0], 2) + min(d[1], GY - d[1])))
+    far = lambda step, count: min(step, count - step)
+    z_steps = sorted(range(1, Z), key=lambda dz: -far(dz, Z))
+    plane_steps = [(dl, dx, dy) for dl in range(X) for dx in range(GX) for dy in range(GY)][1:]
+    plane_steps.sort(key=lambda d: -(d[0] + far(d[1], GX) + far(d[2], GY)))
+
+    def plane_peer(dl, dx, dy):
+        return {"shot": (other if dl else base) + z} | tile_peer(dx, dy)
 
     local = [
         pltpu.make_async_copy(partials.at[0], own, local_sem.at[0]),
@@ -325,18 +324,18 @@
 
     row_a[0:1] = row
     all_a[0:1] = row
-    for n, (dx, dz) in enumerate(shot_steps):
-        send(row_a.at[0:1], all_a.at[n + 1 : n + 2], a_send, a_recv, shot_peer(dx, dz))
+    for n, dz in enumerate(z_steps):
+        send(row_a.at[0:1], all_a.at[n + 1 : n + 2], a_send, a_recv, along_z(dz))
         started.pop()
-    rest_a = all_a.at[1:SHOT]
+    rest_a = all_a.at[1:Z]
     pltpu.make_async_copy(rest_a, rest_a, a_recv).wait()
     row = jnp.sum(all_a[...], axis=0, keepdims=True)
     row_b[0:1] = row
     all_b[0:1] = row
-    for n, (dx, dy) in enumerate(tile_steps):
-        send(row_b.at[0:1], all_b.at[n + 1 : n + 2], b_send, b_recv, tile_peer(dx, dy))
+    for n, d in enumerate(plane_steps):
+        send(row_b.at[0:1], all_b.at[n + 1 : n + 2], b_send, b_recv, plane_peer(*d))
         started.pop()
-    rest_b = all_b.at[1 : GX * GY]
+    rest_b = all_b.at[1 : X * GX * GY]
     pltpu.make_async_copy(rest_b, rest_b, b_recv).wait()
     row = jnp.sum(all_b[...], axis=0, keepdims=True)
 
@@ -399,9 +398,9 @@
             pltpu.VMEM((8, 128), f32),
             pltpu.VMEM((6, 8, 128), f32),
             pltpu.VMEM((8, 128), f32),
-            pltpu.VMEM((SHOT, 128), f32),
+            pltpu.VMEM((Z, 128), f32),
             pltpu.VMEM((8, 128), f32),
-            pltpu.VMEM((GX * GY, 128), f32),
+            pltpu.VMEM((X * GX * GY, 128), f32),
             pltpu.VMEM((SUMS, 128), f32),
             dma((3,)),
             dma((Z,)), dma((Z,)),

time: 49.3 us -> 48.7 us (0.988)
  Pallas kernels: 48.6 us -> 47.9 us
    pallas_call x1, Pallas kernels: 48.6 us -> 47.9 us  [per_device(): pl.pallas_call(kernel, out_shape=jax.ShapeDtypeStruct((3, 1, 8, 128), f32...]
where the time goes in v4:
time: 48.7 us; the launch traced here: 48.6 us
  Pallas kernels  47.9 us (98%)
  local copies, waits for them, and re-layouts  0.6 us (1%)
    pallas_call x1, Pallas kernels, per_device(): pl.pallas_call(kernel, out_shape=jax.ShapeDtypeStruct((3, 1, 8, 128), f32...  47.9 us

profile of v4, /device:TPU:1, one launch (start us, length us, event | category | flops | bytes accessed | tf_op | source)
XLA Modules:
  0.0 48.6 jit_solution(12333456282335010723)
XLA Ops:
  0.0 47.9 %lbfgs_direction.1 = f32[3,1,8,128]{3,2,1,0:T(8,128)S(1)} custom-call(f32[1,9,24,8,128]{4,3,2,1,0:T(8,128)} %partials.1, f32[5,3,1,8,128]{4,3,2,1,0:T(8,128)} %hist_s.1, f32[5,3,1,8,128]{4,3,2,1,0:T(8,128)} %hist_y.1), custom_call_target="tpu_custom_call" | custom-call | tf_op jit(solution)/shard_map/lbfgs_direction/pallas_call | solution.py:384
  48.0 0.6 %copy.5 = f32[3,1,8,128]{3,2,1,0:T(8,128)} copy(f32[3,1,8,128]{3,2,1,0:T(8,128)S(1)} %lbfgs_direction.1) | data formatting | bytes 24576

commit v5 on v4

--- a/solution.py
+++ b/solution.py
@@ -270,7 +270,8 @@
     cols_out[...] = columns
     halo = []
     for n, (dx, dy) in enumerate(((-1, -1), (1, -1), (-1, 1), (1, 1), (0, -1), (0, 1))):
-        halo.append(send(cols_out, cols_in.at[n], halo_send.at[n], halo_recv.at[n], tile_peer(dx, dy)))
+        used = slice(7, 8) if dx > 0 else slice(0, 1) if dx < 0 else slice(0, 8)
+        halo.append(send(cols_out.at[used], cols_in.at[n, used], halo_send.at[n], halo_recv.at[n], tile_peer(dx, dy)))
     halo.append(send(rows_out.at[0, 0:FIELDS], rows_in.at[0, 0:FIELDS], halo_send.at[6], halo_recv.at[6], tile_peer(-1, 0)))
     halo.append(send(rows_out.at[1, 0:FIELDS], rows_in.at[1, 0:FIELDS], halo_send.at[7], halo_recv.at[7], tile_peer(1, 0)))
     for copy in halo:
@@ -336,6 +337,10 @@
         send(row_b.at[0:1], all_b.at[n + 1 : n + 2], b_send, b_recv, plane_peer(*d))
         started.pop()
     rest_b = all_b.at[1 : X * GX * GY]
+    for copy in started:
+        copy.wait_send()
+    pltpu.make_async_copy(rest_a, rest_a, a_send).wait()
+    pltpu.make_async_copy(rest_b, rest_b, b_send).wait()
     pltpu.make_async_copy(rest_b, rest_b, b_recv).wait()
     row = jnp.sum(all_b[...], axis=0, keepdims=True)
 
@@ -370,11 +375,6 @@
         for i in range(PAIRS):
             value = value + wide(coef_q[i]) * s_vec[i][c] - wide(coef_p[i]) * solved[i][c]
         out[c, 0] = -value
-
-    for copy in started:
-        copy.wait_send()
-    pltpu.make_async_copy(rest_a, rest_a, a_send).wait()
-    pltpu.make_async_copy(rest_b, rest_b, b_send).wait()
 
 
 def per_device(partials, hist_s, hist_y):

time: 48.7 us -> 48.6 us (level)
  no operation moved by 1% of the time
where the time goes in v5:
time: 48.6 us; the launch traced here: 48.4 us
  Pallas kernels  47.8 us (98%)
  local copies, waits for them, and re-layouts  0.6 us (1%)
    pallas_call x1, Pallas kernels, per_device(): pl.pallas_call(kernel, out_shape=jax.ShapeDtypeStruct((3, 1, 8, 128), f32...  47.8 us

profile of v5, /device:TPU:1, one launch (start us, length us, event | category | flops | bytes accessed | tf_op | source)
XLA Modules:
  0.0 48.4 jit_solution(10429635847280703232)
XLA Ops:
  0.0 47.8 %lbfgs_direction.1 = f32[3,1,8,128]{3,2,1,0:T(8,128)S(1)} custom-call(f32[1,9,24,8,128]{4,3,2,1,0:T(8,128)} %partials.1, f32[5,3,1,8,128]{4,3,2,1,0:T(8,128)} %hist_s.1, f32[5,3,1,8,128]{4,3,2,1,0:T(8,128)} %hist_y.1), custom_call_target="tpu_custom_call" | custom-call | tf_op jit(solution)/shard_map/lbfgs_direction/pallas_call | solution.py:384
  47.8 0.6 %copy.5 = f32[3,1,8,128]{3,2,1,0:T(8,128)} copy(f32[3,1,8,128]{3,2,1,0:T(8,128)S(1)} %lbfgs_direction.1) | data formatting | bytes 24576
